TPU v7x, 128 devices: a whole 4x4x4 slice. The times are simulated.
128 devices in a mesh: mesh: 8 (over z, core), grid: 16 (over y, x).
Axes of the slice: x: 4, y: 4, z: 4, core: 2. Of those that a mesh axis runs over, the one named last changes fastest.
Arguments:
- mesh_latent: bfloat16 [65536, 512], P(('mesh', 'grid')), may hold values from -6 to 6
- grid_latent: bfloat16 [524288, 512], P(('mesh', 'grid')), may hold values from -6 to 6
- w_send: bfloat16 [512, 512], replicated, may hold values from -0.25 to 0.25
- w_grid: bfloat16 [512, 512], replicated, may hold values from -0.25 to 0.25
- w_agg: bfloat16 [512, 512], replicated, may hold values from -0.25 to 0.25
- w_out: bfloat16 [512, 512], replicated, may hold values from -0.25 to 0.25
- cotangent: bfloat16 [524288, 512], P(('mesh', 'grid')), may hold values from -6 to 6
- tile_mesh: int32 [6144], P(('mesh', 'grid')), may hold values from 0 to 511, as said below
- tile_grid: int32 [6144], P(('mesh', 'grid')), may hold values from 0 to 31, as said below
- tile_count: int32 [128], P(('mesh', 'grid')), may hold values from 24 to 48, as said below
- tile_mask: int32 [6144, 128, 128], P(('mesh', 'grid')), may hold values from 0 to 1
Outputs:
- decoded: bfloat16 [524288, 512], P(('mesh', 'grid'))
- grad_grid: bfloat16 [524288, 512], P(('mesh', 'grid'))
- grad_mesh: bfloat16 [65536, 512], P(('mesh', 'grid'))
- grad_send: float32 [512, 512], replicated
- grad_wgrid: float32 [512, 512], replicated
- grad_wagg: float32 [512, 512], replicated
- grad_wout: float32 [512, 512], replicated
Inputs may be any that keep to these rules, and one draw needn't show every extreme that they name: `tile_mesh`: along the curve order: a tile's mesh block lies in the same index of mesh as its device, and within the blocks of that device or of the device just before or after it along grid; used slots come in order of grid block. `tile_grid`: unused slots hold 0. `tile_count`: some device uses all 48 slots.
All inputs are finite; a program needn't handle non-finite values.
Results may differ from a plain program's by a relative error of at most 0.0095.
Values may be sent and summed in bfloat16 or wider, within the bound.
A program may use at most 192 MiB of HBM per device.

v0:
```python
import functools

import jax
import jax.numpy as jnp
from jax import lax
from jax.experimental import pallas as pl
from jax.experimental.pallas import tpu as pltpu
from jax.sharding import PartitionSpec as P

edge_scale = 0.0625
MESH = pl.DeviceIdType.MESH
MIB = 1024 * 1024
CHUNK = 512
UNROLL = 8
VMEM = pltpu.VMEM
NT = (((1,), (1,)), ((), ()))
TN = (((0,), (0,)), ((), ()))
f32 = jnp.float32
bf16 = jnp.bfloat16
i32 = jnp.int32


def mm(a, b):
    return jnp.dot(a, b, preferred_element_type=f32)


def mm_nt(a, b):
    return lax.dot_general(a, b, NT, preferred_element_type=f32)


def mm_tn(a, b):
    return lax.dot_general(a, b, TN, preferred_element_type=f32)


def silu_parts(v):
    sig = 0.5 * jnp.tanh(0.5 * v) + 0.5
    act = v * sig
    return act, sig + act * (1.0 - sig)


def tile_tables(tile_mesh, tile_grid, tile_count, first, blocks, sources):
    slots = tile_mesh.shape[0]
    order = jnp.arange(slots, dtype=i32)
    live = order < tile_count[0]
    mesh_id = jnp.where(live, tile_mesh - first, sources)
    grid_id = jnp.where(live, tile_grid, blocks)
    same = (grid_id == jnp.roll(grid_id, 1)) & (order > 0)
    each = jnp.arange(blocks, dtype=i32)
    grid_last = jnp.sum((grid_id[None, :] <= each[:, None]).astype(i32), axis=1) - 1
    grid_has = jnp.any(grid_id[None, :] == each[:, None], axis=1)
    ahead = (mesh_id[None, :] < mesh_id[:, None]) | (
        (mesh_id[None, :] == mesh_id[:, None]) & (order[None, :] < order[:, None])
    )
    rank = jnp.sum(ahead.astype(i32), axis=1)
    pick = (rank[None, :] == order[:, None]).astype(i32)

    def ranked(values):
        return jnp.sum(pick * values[None, :], axis=1)

    sorted_mesh = ranked(mesh_id)
    source = jnp.arange(sources, dtype=i32)
    mesh_last = jnp.sum((mesh_id[None, :] <= source[:, None]).astype(i32), axis=1) - 1
    mesh_has = jnp.any(mesh_id[None, :] == source[:, None], axis=1)
    tables = {
        "fwd_mesh": jnp.where(live, mesh_id, 0),
        "fwd_same": same,
        "grid_last": jnp.where(grid_has, grid_last, slots),
        "bwd_slot": ranked(order),
        "bwd_grid": ranked(jnp.where(live, grid_id, 0)),
        "bwd_mesh": jnp.where(sorted_mesh < sources, sorted_mesh, 0),
        "bwd_same": (sorted_mesh == jnp.roll(sorted_mesh, 1)) & (order > 0),
        "mesh_last": jnp.where(mesh_has, mesh_last, slots),
    }
    places, at = {}, 0
    for name, value in tables.items():
        places[name] = at
        at += value.shape[0]
    return places, jnp.concatenate([value.astype(i32) for value in tables.values()])


ORDERS = (("y", "z", "x"), ("z", "y", "x"), ("y", "z", "x"), ("z", "y", "x"))
SEND, WGRID, WAGG, WOUT = 3, 1, 2, 0
SEMS = 20


def decoder_kernel(
    groups,
    places,
    send_scale,
    grid_scale,
    table,
    mesh_hbm,
    grid_hbm,
    cot_hbm,
    mask_hbm,
    wsend_hbm,
    wgrid_hbm,
    wagg_hbm,
    wout_hbm,
    dec_hbm,
    gg_hbm,
    gm_ref,
    final,
    grid_v,
    cot_v,
    pre_v,
    dpre_v,
    hidden_v,
    dagg_v,
    src_v,
    panels,
    slope,
    mask_i,
    mask_v,
    wsend_v,
    wgrid_v,
    wagg_v,
    wout_v,
    runs,
    total,
    acc_out,
    acc_t,
    ds_v,
    ds_in,
    packed,
    r0,
    r1,
    r2,
    r3,
    a1,
    b1,
    load_sem,
    chunk_sem,
    mask_sem,
    out_sem,
    halo_send,
    halo_recv,
    send_sem,
    recv_sem,
):
    slots, block, _ = mask_v.shape
    rows, width = mesh_hbm.shape
    grid_rows = grid_v.shape[0]
    chunks = grid_rows // CHUNK
    row = lax.axis_index("mesh")
    col = lax.axis_index("grid")
    core = lax.rem(row, 2)
    at = {"z": row // 2, "y": col // 4, "x": lax.rem(col, 4)}
    left = (row, lax.rem(col + groups - 1, groups))
    right = (row, lax.rem(col + 1, groups))
    sibling = (row + 1 - 2 * core, col)

    def peer(axis, d):
        to = lax.rem(at[axis] + d, 4)
        if axis == "z":
            return (to * 2 + core, col)
        if axis == "y":
            return (row, to * 4 + at["x"])
        return (row, at["y"] * 4 + to)

    def entry(name, index):
        return table[places[name] + index]

    barrier = pltpu.get_barrier_semaphore()
    others = [left, right, sibling] + [peer(axis, d) for axis in "xyz" for d in (1, 2, 3)]
    for other in others:
        pl.semaphore_signal(barrier, inc=1, device_id=other, device_id_type=MESH)
    loads = [
        pltpu.make_async_copy(src, dst, load_sem.at[k])
        for k, (src, dst) in enumerate(
            (
                (wgrid_hbm, wgrid_v),
                (wout_hbm, wout_v),
                (mesh_hbm, src_v.at[pl.ds(rows, rows)]),
                (wsend_hbm, wsend_v),
                (wagg_hbm, wagg_v),
            )
        )
    ]

    def chunk_loads(c):
        part = pl.ds(pl.multiple_of(c * CHUNK, CHUNK), CHUNK)
        return (
            pltpu.make_async_copy(grid_hbm.at[part], grid_v.at[part], chunk_sem.at[0, c]),
            pltpu.make_async_copy(cot_hbm.at[part], cot_v.at[part], chunk_sem.at[1, c]),
        )

    loads[0].start()
    loads[1].start()
    for copy in chunk_loads(0):
        copy.start()
    pl.semaphore_wait(barrier, len(others))
    halos = [
        pltpu.make_async_remote_copy(
            src_ref=mesh_hbm,
            dst_ref=src_v.at[pl.ds(2 * slot * rows, rows)],
            send_sem=halo_send.at[slot],
            recv_sem=halo_recv.at[slot],
            device_id=to,
            device_id_type=MESH,
        )
        for slot, to in enumerate((right, left))
    ]
    for copy in halos:
        copy.start()
    for c in range(1, chunks):
        for copy in chunk_loads(c):
            copy.start()
    for copy in loads[2:]:
        copy.start()
    quarter = mask_i.shape[0]
    masks = [
        pltpu.make_async_copy(mask_hbm.at[pl.ds(q * quarter, quarter)], mask_i, mask_sem)
        for q in range(slots // quarter)
    ]
    masks[0].start()

    loads[0].wait()
    loads[1].wait()

    def early(c, carry):
        for copy in chunk_loads(c):
            copy.wait()
        part = pl.ds(pl.multiple_of(c * CHUNK, CHUNK), CHUNK)
        pre_v[part, :] = mm(grid_v[part, :], wgrid_v[...])
        dpre_v[part, :] = mm_nt(cot_v[part, :], wout_v[...]).astype(bf16)
        return carry

    lax.fori_loop(0, chunks, early, 0)
    for copy in loads[2:]:
        copy.wait()

    per_part = rows // block

    def project(part):
        where = pl.ds(part * rows, rows)
        act, grad = silu_parts(mm(src_v[where, :], wsend_v[...]))
        blocks = pl.ds(part * per_part, per_part)
        panels[blocks] = act.astype(bf16).reshape(per_part, block, width)
        slope[blocks] = grad.reshape(per_part, block, width)

    project(1)
    for q, copy in enumerate(masks):
        copy.wait()

        def convert(k, carry, q=q):
            t = q * quarter + k
            mask_v[t] = mask_i[k].astype(f32).astype(bf16)
            return carry

        lax.fori_loop(0, quarter, convert, 0)
        if q + 1 < len(masks):
            masks[q + 1].start()
    acc_out[...] = jnp.zeros_like(acc_out)
    acc_t[...] = jnp.zeros_like(acc_t)
    total[...] = jnp.zeros_like(total)
    runs[slots] = jnp.zeros((block, width), bf16)
    for copy in halos:
        copy.wait()
    project(0)
    project(2)

    def forward(outer, carry):
        for inner in range(UNROLL):
            t = outer * UNROLL + inner
            keep = entry("fwd_same", t).astype(f32)
            value = total[...] * keep + mm(mask_v[t], panels[entry("fwd_mesh", t)])
            total[...] = value
            runs[t] = (value * edge_scale).astype(bf16)
        return carry

    lax.fori_loop(0, slots // UNROLL, forward, 0)

    def looked_up(last, index):
        return runs[entry(last, index)]

    per_chunk = CHUNK // block

    def node_mlp(c, carry):
        part = pl.ds(pl.multiple_of(c * CHUNK, CHUNK), CHUNK)
        agg = jnp.concatenate(
            [looked_up("grid_last", c * per_chunk + k) for k in range(per_chunk)], axis=0
        )
        act, grad = silu_parts(pre_v[part, :] + mm(agg, wagg_v[...]))
        hidden = act.astype(bf16)
        hidden_v[part, :] = hidden
        dpre = (dpre_v[part, :].astype(f32) * grad).astype(bf16)
        dpre_v[part, :] = dpre
        dagg = mm_nt(dpre, wagg_v[...]).astype(bf16)
        dagg_v[pl.ds(c * per_chunk, per_chunk)] = dagg.reshape(per_chunk, block, width)
        acc_out[...] += mm_tn(hidden, cot_v[part, :])
        dpre_t = dpre.T
        acc_t[:, :width] += mm(dpre_t, grid_v[part, :])
        acc_t[:, width:] += mm(dpre_t, agg)
        return carry

    lax.fori_loop(0, chunks, node_mlp, 0)

    half = packed.shape[1] // 2
    first_size, second_size = half // 4, half // 16
    mine = pl.multiple_of(core * half, half)
    theirs = pl.multiple_of((1 - core) * half, half)
    started = []

    def go(src, dst, sem, to):
        copy = pltpu.make_async_remote_copy(
            src_ref=src,
            dst_ref=dst,
            send_sem=send_sem.at[sem],
            recv_sem=recv_sem.at[sem],
            device_id=to,
            device_id_type=MESH,
        )
        copy.start()
        started.append(copy)
        return copy

    def fill(i, value, scale):
        for c in range(width // 128):
            packed[i, pl.ds(c * width, width), :] = (value[:, c * 128 : (c + 1) * 128] * scale).astype(bf16)

    def arrived(copies):
        for copy in copies:
            copy.wait_recv()

    def stream(i):
        axis_a, axis_b, axis_c = ORDERS[i]
        sem = i * SEMS
        copies = [go(packed.at[i, pl.ds(theirs, half)], r0.at[i], sem, sibling)]
        yield
        arrived(copies)
        off_a = pl.multiple_of(at[axis_a] * first_size, first_size)
        own = pl.multiple_of(mine + off_a, first_size)
        a1[i] = packed[i, pl.ds(own, first_size), :].astype(f32) + r0[i, pl.ds(off_a, first_size), :].astype(f32)
        r0[i] = (packed[i, pl.ds(mine, half), :].astype(f32) + r0[i].astype(f32)).astype(bf16)

        def scatter(source, target, axis, size, sem):
            return [
                go(
                    source.at[i, pl.ds(pl.multiple_of(lax.rem(at[axis] + d, 4) * size, size), size)],
                    target.at[i, d - 1],
                    sem + d,
                    peer(axis, d),
                )
                for d in (1, 2, 3)
            ]

        copies = scatter(r0, r1, axis_a, first_size, sem)
        yield
        arrived(copies)
        value = a1[i]
        for d in range(3):
            value = value + r1[i, d].astype(f32)
        a1[i] = value
        b1[i] = value.astype(bf16)
        copies = scatter(b1, r2, axis_b, second_size, sem + 3)
        yield
        arrived(copies)
        off_b = pl.multiple_of(at[axis_b] * second_size, second_size)
        value = a1[i, pl.ds(off_b, second_size), :]
        for d in range(3):
            value = value + r2[i, d].astype(f32)
        me = at[axis_c]
        r3[i, me] = value.astype(bf16)
        copies = [go(r3.at[i, me], r3.at[i, me], sem + 6 + d, peer(axis_c, d)) for d in (1, 2, 3)]
        yield
        arrived(copies)
        value = r3[i, 0].astype(f32)
        for k in range(1, 4):
            value = value + r3[i, k].astype(f32)
        place = pl.multiple_of(mine + off_a + off_b, second_size)
        final[i, pl.ds(place, second_size), :] = value.astype(bf16)

        def gather(place, size, axis, sem):
            window = final.at[i, pl.ds(place, size)]
            return [go(window, window, sem + d, peer(axis, d)) for d in (1, 2, 3)]

        copies = gather(place, second_size, axis_b, sem + 9)
        yield
        arrived(copies)
        copies = gather(own, first_size, axis_a, sem + 12)
        yield
        arrived(copies)
        window = final.at[i, pl.ds(mine, half)]
        copies = [go(window, window, sem + 16, sibling)]
        yield
        arrived(copies)

    streams = [stream(i) for i in range(4)]

    def advance(*which):
        for i in which:
            next(streams[i], None)

    fill(WOUT, acc_out[...], grid_scale)
    advance(WOUT)
    fill(WGRID, acc_t[:, :width].T, grid_scale)
    advance(WGRID)
    fill(WAGG, acc_t[:, width:].T, grid_scale)
    advance(WAGG)

    total[...] = jnp.zeros_like(total)

    def backward(outer, carry):
        for inner in range(UNROLL):
            r = outer * UNROLL + inner
            keep = entry("bwd_same", r).astype(f32)
            value = total[...] * keep + mm_tn(mask_v[entry("bwd_slot", r)], dagg_v[entry("bwd_grid", r)])
            total[...] = value
            runs[r] = (value * edge_scale * slope[entry("bwd_mesh", r)]).astype(bf16)
        return carry

    steps = slots // UNROLL
    lax.fori_loop(0, 3, backward, 0)
    advance(WOUT, WGRID, WAGG)
    lax.fori_loop(3, steps, backward, 0)
    for b in range(ds_v.shape[0] // block):
        ds_v[pl.ds(b * block, block), :] = looked_up("mesh_last", b)
    returns = [
        pltpu.make_async_remote_copy(
            src_ref=ds_v.at[pl.ds(2 * slot * rows, rows)],
            dst_ref=ds_in.at[slot],
            send_sem=halo_send.at[2 + slot],
            recv_sem=halo_recv.at[2 + slot],
            device_id=to,
            device_id_type=MESH,
        )
        for slot, to in enumerate((left, right))
    ]
    for copy in returns:
        copy.start()
    fill(SEND, mm_tn(src_v[...], ds_v[...]), send_scale)
    advance(SEND)

    def finish_chunk(c):
        part = pl.ds(c * CHUNK, CHUNK)
        dec = grid_v[part, :].astype(f32) + mm(hidden_v[part, :], wout_v[...])
        hidden_v[part, :] = dec.astype(bf16)
        out = pltpu.make_async_copy(hidden_v.at[part], dec_hbm.at[part], out_sem.at[0, c])
        out.start()
        gg = cot_v[part, :].astype(f32) + mm_nt(dpre_v[part, :], wgrid_v[...])
        dpre_v[part, :] = gg.astype(bf16)
        out_g = pltpu.make_async_copy(dpre_v.at[part], gg_hbm.at[part], out_sem.at[1, c])
        out_g.start()
        return [out, out_g]

    outs = []
    for c in range(chunks):
        outs += finish_chunk(c)
        if c == 1:
            advance(SEND)
        if c == 4:
            advance(WOUT, WGRID, WAGG)
    for _ in range(3):
        advance(SEND)
        advance(WOUT, WGRID, WAGG)
    for copy in returns:
        copy.wait()
    dsender = ds_v[pl.ds(rows, rows), :].astype(f32) + ds_in[0].astype(f32) + ds_in[1].astype(f32)
    gm_ref[...] = mm_nt(dsender.astype(bf16), wsend_v[...]).astype(bf16)
    for _ in range(8):
        advance(SEND, WOUT, WGRID, WAGG)
    for copy in outs:
        copy.wait()
    for copy in started:
        copy.wait_send()


def decoder_call(groups, places, send_scale, grid_scale, table, *arrays):
    mesh_latent, grid_latent, _, tile_mask = arrays[:4]
    slots, block, _ = tile_mask.shape
    rows, width = mesh_latent.shape
    grid_rows = grid_latent.shape[0]
    full = width * width // 128
    half = full // 2
    vspec = pl.BlockSpec(memory_space=VMEM)
    hspec = pl.BlockSpec(memory_space=pltpu.HBM)
    dma = pltpu.SemaphoreType.DMA
    weight = VMEM((width, width), bf16)
    node = VMEM((grid_rows, width), bf16)
    chunks = grid_rows // CHUNK
    return pl.pallas_call(
        functools.partial(decoder_kernel, groups, places, send_scale, grid_scale),
        name="decoder",
        out_shape=[
            jax.ShapeDtypeStruct((grid_rows, width), bf16),
            jax.ShapeDtypeStruct((grid_rows, width), bf16),
            jax.ShapeDtypeStruct((rows, width), bf16),
            jax.ShapeDtypeStruct((4, full, 128), bf16),
        ],
        in_specs=[pl.BlockSpec(memory_space=pltpu.SMEM)] + [hspec] * 8,
        out_specs=[hspec, hspec, vspec, vspec],
        scratch_shapes=[
            node,
            node,
            VMEM((grid_rows, width), f32),
            node,
            node,
            VMEM((grid_rows // block, block, width), bf16),
            VMEM((3 * rows, width), bf16),
            VMEM((3 * rows // block, block, width), bf16),
            VMEM((3 * rows // block, block, width), f32),
            VMEM((slots // 4, block, block), i32),
            VMEM((slots, block, block), bf16),
            weight,
            weight,
            weight,
            weight,
            VMEM((slots + 1, block, width), bf16),
            VMEM((block, width), f32),
            VMEM((width, width), f32),
            VMEM((width, 2 * width), f32),
            VMEM((3 * rows, width), bf16),
            VMEM((2, rows, width), bf16),
            VMEM((4, full, 128), bf16),
            VMEM((4, half, 128), bf16),
            VMEM((4, 3, half // 4, 128), bf16),
            VMEM((4, 3, half // 16, 128), bf16),
            VMEM((4, 4, half // 16, 128), bf16),
            VMEM((4, half // 4, 128), f32),
            VMEM((4, half // 4, 128), bf16),
            dma((5,)),
            dma((2, chunks)),
            dma,
            dma((2, chunks)),
            dma((4,)),
            dma((4,)),
            dma((4 * SEMS,)),
            dma((4 * SEMS,)),
        ],
        compiler_params=pltpu.CompilerParams(
            collective_id=0, has_side_effects=True, vmem_limit_bytes=61 * MIB
        ),
    )(table, *arrays)


def finish_kernel(packed_ref, *grads):
    width = grads[0].shape[0]
    for index, out in enumerate(grads):
        for c in range(width // 128):
            out[:, c * 128 : (c + 1) * 128] = packed_ref[index, pl.ds(c * width, width), :].astype(f32)


def finish_call(packed, width):
    vspec = pl.BlockSpec(memory_space=VMEM)
    return pl.pallas_call(
        finish_kernel,
        name="finish",
        out_shape=[jax.ShapeDtypeStruct((width, width), f32)] * 4,
        in_specs=[vspec],
        out_specs=[vspec] * 4,
        compiler_params=pltpu.CompilerParams(vmem_limit_bytes=32 * MIB),
    )(packed)


def per_device(
    mesh_latent,
    grid_latent,
    w_send,
    w_grid,
    w_agg,
    w_out,
    cotangent,
    tile_mesh,
    tile_grid,
    tile_count,
    tile_mask,
):
    block = tile_mask.shape[1]
    mesh_rows, width = mesh_latent.shape
    grid_rows = grid_latent.shape[0]
    groups = lax.axis_size("grid")
    devices_all = lax.axis_size("mesh") * groups
    send_scale = (mesh_rows * devices_all) ** (-0.5)
    grid_scale = (grid_rows * devices_all) ** (-0.5)
    mesh_blocks = mesh_rows // block
    first = (lax.axis_index("mesh") * groups + lax.axis_index("grid") - 1) * mesh_blocks
    places, table = tile_tables(
        tile_mesh, tile_grid, tile_count, first, grid_rows // block, 3 * mesh_blocks
    )
    decoded, grad_grid, grad_mesh, final = decoder_call(
        groups,
        places,
        send_scale,
        grid_scale,
        table,
        mesh_latent,
        grid_latent,
        cotangent,
        tile_mask,
        w_send,
        w_grid,
        w_agg,
        w_out,
    )
    grads = finish_call(final, width)
    return (decoded, grad_grid, grad_mesh, grads[SEND], grads[WGRID], grads[WAGG], grads[WOUT])


def solution(mesh):
    both = ("mesh", "grid")
    return jax.shard_map(
        per_device,
        mesh=mesh,
        in_specs=(
            P(both, None),
            P(both, None),
            P(),
            P(),
            P(),
            P(),
            P(both, None),
            P(both),
            P(both),
            P(both),
            P(both, None, None),
        ),
        out_specs=(P(both, None), P(both, None), P(both, None), P(), P(), P(), P()),
        check_vma=False,
    )
```

profile of v0, /device:TPU:1, one launch (start us, length us, event | category | flops | bytes accessed | tf_op | source)
XLA Modules:
  0.0 102.1 jit_solution(17835833189846463364)
XLA Ops:
  1.3 0.7 fusion.4
  2.0 0.6 slice.14
  2.5 0.7 and_convert_fusion.1
  3.3 0.2 convert_reduce_fusion
  3.4 0.1 convert_reduce_fusion.2
  3.6 0.1 fusion.3
  3.7 0.2 select_reduce_fusion
  3.8 0.6 slice.16
  4.4 0.7 and_convert_fusion
  5.2 0.1 convert_reduce_fusion.1
  5.3 0.1 fusion.2
  5.4 0.7 concatenate.12.table
  6.1 84.6 %decoder.1 = (bf16[4096,512]{1,0:T(8,128)(2,1)}, bf16[4096,512]{1,0:T(8,128)(2,1)}, bf16[512,512]{1,0:T(8,128)(2,1)}, bf16[4,2048,128]{2,1,0:T(8,128)(2,1)}) custom-call(s32[332]{0:T(512)} %concatenate.12.table, bf16[512,512]{1,0:T(8,128)(2,1)} %mesh_hbm.1, bf16[4096,512]{1,0:T(8,128)(2,1)} %grid_hbm.1, bf16[4096,512]{1,0:T(8,128)(2,1)} %cot_hbm.1, ...), custom_call_target="tpu_custom_call" | custom-call | tf_op jit(solution)/shard_map/decoder/pallas_call | solution.py:482
  90.7 0.0 copy-start
  90.7 1.6 %copy-done = bf16[4,2048,128]{2,1,0:T(8,128)(2,1)S(1)} copy-done((bf16[4,2048,128]{2,1,0:T(8,128)(2,1)S(1)}, bf16[4,2048,128]{2,1,0:T(8,128)(2,1)}, u32[]{:S(2)}) %copy-start) | copy-done | bytes 2097176
  92.3 2.4 %finish.1 = (f32[512,512]{1,0:T(8,128)}, f32[512,512]{1,0:T(8,128)}, f32[512,512]{1,0:T(8,128)}, f32[512,512]{1,0:T(8,128)}) custom-call(bf16[4,2048,128]{2,1,0:T(8,128)(2,1)S(1)} %copy-done), custom_call_target="tpu_custom_call" | custom-call | tf_op jit(solution)/shard_map/finish/pallas_call | solution.py:546
  94.7 0.0 copy-start.1
  94.7 4.6 %copy.22 = bf16[4096,512]{1,0:T(8,128)(2,1)} copy(bf16[4096,512]{1,0:T(8,128)(2,1)} %get-tuple-element.39) | data formatting | bytes 8388608
  99.3 0.0 copy-done.1
  99.3 0.0 copy-start.2
  99.3 2.0 %copy.23 = bf16[4096,512]{1,0:T(8,128)(2,1)} copy(bf16[4096,512]{1,0:T(8,128)(2,1)S(1)} %copy-done.1) | data formatting | bytes 8388608
  101.3 0.0 copy-done.2
  101.3 0.8 copy.24
  (3 shorter events, 0.0 us)
Async XLA Ops:
  90.7 1.6 %copy-start = (bf16[4,2048,128]{2,1,0:T(8,128)(2,1)S(1)}, bf16[4,2048,128]{2,1,0:T(8,128)(2,1)}, u32[]{:S(2)}) copy-start(bf16[4,2048,128]{2,1,0:T(8,128)(2,1)} %get-tuple-element.18.packed_ref) | copy-start | bytes 6291460
  94.7 4.6 %copy-start.1 = (bf16[4096,512]{1,0:T(8,128)(2,1)S(1)}, bf16[4096,512]{1,0:T(8,128)(2,1)}, u32[]{:S(2)}) copy-start(bf16[4096,512]{1,0:T(8,128)(2,1)} %get-tuple-element.40) | copy-start | bytes 12582916
  99.3 2.0 %copy-start.2 = (bf16[512,512]{1,0:T(8,128)(2,1)S(1)}, bf16[512,512]{1,0:T(8,128)(2,1)}, u32[]{:S(2)}) copy-start(bf16[512,512]{1,0:T(8,128)(2,1)} %get-tuple-element.41) | copy-start | bytes 1572868
where the time goes:
time: 102 us
  Pallas kernels  87 us (85%)
  local copies, waits for them, and re-layouts  10.9 us (11%)
  other arithmetic  2.91 us (3%)
  between operations  1.33 us (1%)
    pallas_call x1, Pallas kernels, decoder_call(): pl.pallas_call(functools.partial(decoder_kernel, groups, places, send_sca...  84.6 us
    unnamed x9, local copies, waits for them, and re-layouts  9.03 us
    pallas_call x1, Pallas kernels, finish_call(): pl.pallas_call(finish_kernel, name='finish', out_shape=[jax.ShapeDtypeStr...  2.36 us

commit v1 on v0

v1 whole, which is shorter than its diff:
```python
import functools

import jax
import jax.numpy as jnp
from jax import lax
from jax.experimental import pallas as pl
from jax.experimental.pallas import tpu as pltpu
from jax.sharding import PartitionSpec as P

edge_scale = 0.0625
MESH = pl.DeviceIdType.MESH
MIB = 1024 * 1024
CHUNK = 512
UNROLL = 8
VMEM = pltpu.VMEM
NT = (((1,), (1,)), ((), ()))
TN = (((0,), (0,)), ((), ()))
f32 = jnp.float32
bf16 = jnp.bfloat16
i32 = jnp.int32


def mm(a, b):
    return jnp.dot(a, b, preferred_element_type=f32)


def mm_nt(a, b):
    return lax.dot_general(a, b, NT, preferred_element_type=f32)


def mm_tn(a, b):
    return lax.dot_general(a, b, TN, preferred_element_type=f32)


def silu_parts(v):
    sig = 0.5 * jnp.tanh(0.5 * v) + 0.5
    act = v * sig
    return act, sig + act * (1.0 - sig)


ROWS = {
    "fwd_mesh": 0,
    "fwd_same": 1,
    "grid_last": 2,
    "bwd_slot": 3,
    "bwd_grid": 4,
    "bwd_mesh": 5,
    "bwd_same": 6,
    "mesh_last": 7,
}


def tile_tables(tmesh, tgrid, tcount, first, blocks, sources, mesh_col, grid_col, out):
    slots = tmesh.shape[0]
    for t in range(slots):
        mesh_col[t : t + 1, :] = jnp.full((1, 128), tmesh[t], i32)
        grid_col[t : t + 1, :] = jnp.full((1, 128), tgrid[t], i32)
    shape = (slots, 128)
    sub = lax.broadcasted_iota(i32, shape, 0)
    lane = lax.broadcasted_iota(i32, shape, 1)
    live = sub < tcount[0]
    key = jnp.where(live, mesh_col[...] - first, sources)
    gid = jnp.where(live, grid_col[...], blocks)

    def down(mask, values):
        return jnp.sum(jnp.where(mask, values, 0), axis=0, keepdims=True)

    one = jnp.ones(shape, i32)
    diag = sub == lane
    later = lane[0:1, :] > 0
    key_row = down(diag, key)
    ahead = ((key_row < key) | ((key_row == key) & (lane < sub))) & (lane < slots)
    rank = jnp.sum(jnp.where(ahead, one, 0), axis=1, keepdims=True)
    pick = rank == lane
    sorted_key = down(pick, key)
    same_key = (sorted_key == down(rank == lane - 1, key)) & later
    grid_row = down(diag, gid)
    same_grid = (grid_row == down(sub == lane - 1, gid)) & later
    rows = {
        "fwd_mesh": down(diag & live, key),
        "fwd_same": same_grid.astype(i32),
        "grid_last": jnp.where(down(gid == lane, one) > 0, down(gid <= lane, one) - 1, slots),
        "bwd_slot": down(pick, sub),
        "bwd_grid": down(pick & live, gid),
        "bwd_mesh": jnp.where(sorted_key < sources, sorted_key, 0),
        "bwd_same": same_key.astype(i32),
        "mesh_last": jnp.where(down(key == lane, one) > 0, down(key <= lane, one) - 1, slots),
    }
    for name, value in rows.items():
        out[ROWS[name] : ROWS[name] + 1, :] = value


PLANE = tuple((dy, dz) for dy in range(4) for dz in range(4) if (dy, dz) != (0, 0))
SEND, WGRID, WAGG, WOUT = 3, 1, 2, 0
SEMS = 35
PIECES = 4


def decoder_kernel(
    groups,
    send_scale,
    grid_scale,
    tmesh,
    tgrid,
    tcount,
    mesh_hbm,
    grid_hbm,
    cot_hbm,
    mask_hbm,
    wsend_hbm,
    wgrid_hbm,
    wagg_hbm,
    wout_hbm,
    dec_hbm,
    gg_hbm,
    gm_hbm,
    final_hbm,
    grid_v,
    cot_v,
    pre_v,
    dpre_v,
    hidden_v,
    dagg_v,
    src_v,
    panels,
    slope,
    mask_i,
    mask_v,
    wsend_v,
    wgrid_v,
    wagg_v,
    wout_v,
    runs,
    total,
    acc_out,
    acc_t,
    ds_v,
    ds_in,
    packed,
    final,
    r0,
    r1,
    r3,
    gm_v,
    mesh_col,
    grid_col,
    table_v,
    table,
    load_sem,
    chunk_sem,
    mask_sem,
    table_sem,
    out_sem,
    end_sem,
    halo_send,
    halo_recv,
    send_sem,
    recv_sem,
):
    slots, block, _ = mask_v.shape
    rows, width = mesh_hbm.shape
    grid_rows = grid_v.shape[0]
    chunks = grid_rows // CHUNK
    row = lax.axis_index("mesh")
    col = lax.axis_index("grid")
    core = lax.rem(row, 2)
    at = {"z": row // 2, "y": col // 4, "x": lax.rem(col, 4)}
    left = (row, lax.rem(col + groups - 1, groups))
    right = (row, lax.rem(col + 1, groups))
    sibling = (row + 1 - 2 * core, col)

    def plane(dy, dz):
        to_y, to_z = lax.rem(at["y"] + dy, 4), lax.rem(at["z"] + dz, 4)
        return (to_z * 2 + core, to_y * 4 + at["x"]), to_y * 4 + to_z

    def along_x(d):
        return (row, at["y"] * 4 + lax.rem(at["x"] + d, 4))

    def entry(name, index):
        return table[ROWS[name], index]

    barrier = pltpu.get_barrier_semaphore()
    others = [left, right, sibling] + [along_x(d) for d in (1, 2, 3)] + [plane(*step)[0] for step in PLANE]
    for other in others:
        pl.semaphore_signal(barrier, inc=1, device_id=other, device_id_type=MESH)
    loads = [
        pltpu.make_async_copy(src, dst, load_sem.at[k])
        for k, (src, dst) in enumerate(
            (
                (wgrid_hbm, wgrid_v),
                (wout_hbm, wout_v),
                (mesh_hbm, src_v.at[pl.ds(rows, rows)]),
                (wsend_hbm, wsend_v),
                (wagg_hbm, wagg_v),
            )
        )
    ]

    def chunk_loads(c):
        part = pl.ds(pl.multiple_of(c * CHUNK, CHUNK), CHUNK)
        return (
            pltpu.make_async_copy(grid_hbm.at[part], grid_v.at[part], chunk_sem.at[0, c]),
            pltpu.make_async_copy(cot_hbm.at[part], cot_v.at[part], chunk_sem.at[1, c]),
        )

    quarter = mask_i.shape[1]
    masks = [
        pltpu.make_async_copy(mask_hbm.at[pl.ds(q * quarter, quarter)], mask_i.at[q % 2], mask_sem.at[q % 2])
        for q in range(slots // quarter)
    ]
    loads[0].start()
    loads[1].start()
    masks[0].start()
    for copy in chunk_loads(0):
        copy.start()
    pl.semaphore_wait(barrier, len(others))
    halos = [
        pltpu.make_async_remote_copy(
            src_ref=mesh_hbm,
            dst_ref=src_v.at[pl.ds(2 * slot * rows, rows)],
            send_sem=halo_send.at[slot],
            recv_sem=halo_recv.at[slot],
            device_id=to,
            device_id_type=MESH,
        )
        for slot, to in enumerate((right, left))
    ]
    for copy in halos:
        copy.start()
    masks[1].start()
    for c in range(1, chunks):
        for copy in chunk_loads(c):
            copy.start()
    for copy in loads[2:]:
        copy.start()
    loads[0].wait()
    loads[1].wait()

    def early(c, carry):
        for copy in chunk_loads(c):
            copy.wait()
        part = pl.ds(pl.multiple_of(c * CHUNK, CHUNK), CHUNK)
        pre_v[part, :] = mm(grid_v[part, :], wgrid_v[...])
        dpre_v[part, :] = mm_nt(cot_v[part, :], wout_v[...]).astype(bf16)
        return carry

    lax.fori_loop(0, chunks, early, 0)
    for copy in loads[2:]:
        copy.wait()

    per_part = rows // block

    def project(part):
        where = pl.ds(part * rows, rows)
        act, grad = silu_parts(mm(src_v[where, :], wsend_v[...]))
        blocks = pl.ds(part * per_part, per_part)
        panels[blocks] = act.astype(bf16).reshape(per_part, block, width)
        slope[blocks] = grad.reshape(per_part, block, width)

    project(1)
    per_grid = grid_rows // block
    first = (row * groups + col - 1) * per_part
    tile_tables(tmesh, tgrid, tcount, first, per_grid, 3 * per_part, mesh_col, grid_col, table_v)
    to_scalars = pltpu.make_async_copy(table_v, table, table_sem)
    to_scalars.start()
    for q, copy in enumerate(masks):
        copy.wait()

        def convert(k, carry, q=q):
            t = q * quarter + k
            mask_v[t] = mask_i[q % 2, k].astype(f32).astype(bf16)
            return carry

        lax.fori_loop(0, quarter, convert, 0)
        if q + 2 < len(masks):
            masks[q + 2].start()
    acc_out[...] = jnp.zeros_like(acc_out)
    acc_t[...] = jnp.zeros_like(acc_t)
    total[...] = jnp.zeros_like(total)
    runs[slots] = jnp.zeros((block, width), bf16)
    to_scalars.wait()
    for copy in halos:
        copy.wait()
    project(0)
    project(2)

    def forward(outer, carry):
        for inner in range(UNROLL):
            t = outer * UNROLL + inner
            keep = entry("fwd_same", t).astype(f32)
            value = total[...] * keep + mm(mask_v[t], panels[entry("fwd_mesh", t)])
            total[...] = value
            runs[t] = (value * edge_scale).astype(bf16)
        return carry

    lax.fori_loop(0, slots // UNROLL, forward, 0)

    def looked_up(last, index):
        return runs[entry(last, index)]

    per_chunk = CHUNK // block

    def agg_chunk(c):
        return jnp.concatenate([looked_up("grid_last", c * per_chunk + k) for k in range(per_chunk)], axis=0)

    def node_mlp(c, carry):
        part = pl.ds(pl.multiple_of(c * CHUNK, CHUNK), CHUNK)
        act, grad = silu_parts(pre_v[part, :] + mm(agg_chunk(c), wagg_v[...]))
        hidden = act.astype(bf16)
        hidden_v[part, :] = hidden
        dpre_v[part, :] = (dpre_v[part, :].astype(f32) * grad).astype(bf16)
        acc_out[...] += mm_tn(hidden, cot_v[part, :])
        return carry

    def input_grads(c, carry):
        part = pl.ds(pl.multiple_of(c * CHUNK, CHUNK), CHUNK)
        dpre_t = dpre_v[part, :].T
        acc_t[:, :width] += mm(dpre_t, grid_v[part, :])
        acc_t[:, width:] += mm(dpre_t, agg_chunk(c))
        return carry

    def agg_grads(c, carry):
        part = pl.ds(pl.multiple_of(c * CHUNK, CHUNK), CHUNK)
        dagg = mm_nt(dpre_v[part, :], wagg_v[...]).astype(bf16)
        dagg_v[pl.ds(c * per_chunk, per_chunk)] = dagg.reshape(per_chunk, block, width)
        return carry

    half = packed.shape[1] // 2
    size = half // 16
    place = pl.multiple_of((at["y"] * 4 + at["z"]) * size, size)
    mine = pl.multiple_of(core * half, half)
    theirs = pl.multiple_of((1 - core) * half, half)
    own = pl.multiple_of(mine + place, size)
    started = []

    def go(src, dst, sem, to):
        copy = pltpu.make_async_remote_copy(
            src_ref=src,
            dst_ref=dst,
            send_sem=send_sem.at[sem],
            recv_sem=recv_sem.at[sem],
            device_id=to,
            device_id_type=MESH,
        )
        copy.start()
        started.append(copy)
        return copy

    def fill(i, value, scale):
        for c in range(width // 128):
            packed[i, pl.ds(c * width, width), :] = (value[:, c * 128 : (c + 1) * 128] * scale).astype(bf16)

    def arrived(copies):
        for copy in copies:
            copy.wait_recv()

    def stream(i):
        sem = i * SEMS
        copies = [go(packed.at[i, pl.ds(theirs, half)], r0.at[i], sem, sibling)]
        yield
        arrived(copies)
        chunk = packed[i, pl.ds(own, size), :].astype(f32) + r0[i, pl.ds(place, size), :].astype(f32)
        r0[i] = (packed[i, pl.ds(mine, half), :].astype(f32) + r0[i].astype(f32)).astype(bf16)
        copies = []
        for k, step in enumerate(PLANE):
            to, index = plane(*step)
            window = pl.ds(pl.multiple_of(index * size, size), size)
            copies.append(go(r0.at[i, window], r1.at[i, k], sem + 1 + k, to))
        yield
        arrived(copies)
        for k in range(len(PLANE)):
            chunk = chunk + r1[i, k].astype(f32)
        me = at["x"]
        r3[i, me] = chunk.astype(bf16)
        copies = [go(r3.at[i, me], r3.at[i, me], sem + 15 + d, along_x(d)) for d in (1, 2, 3)]
        yield
        arrived(copies)
        value = r3[i, 0].astype(f32)
        for k in range(1, 4):
            value = value + r3[i, k].astype(f32)
        final[i, pl.ds(own, size), :] = value.astype(bf16)
        window = final.at[i, pl.ds(own, size)]
        copies = [go(window, window, sem + 19 + k, plane(*step)[0]) for k, step in enumerate(PLANE)]
        yield
        arrived(copies)
        window = final.at[i, pl.ds(mine, half)]
        copies = [go(window, window, sem + 34, sibling)]
        yield
        arrived(copies)
        out = pltpu.make_async_copy(final.at[i], final_hbm.at[i], end_sem.at[i])
        out.start()
        outs.append(out)

    outs = []
    streams = [stream(i) for i in range(4)]

    def advance(*which):
        for i in which:
            next(streams[i], None)

    lax.fori_loop(0, chunks, node_mlp, 0)
    fill(WOUT, acc_out[...], grid_scale)
    advance(WOUT)
    lax.fori_loop(0, chunks // 2, input_grads, 0)
    advance(WOUT)
    lax.fori_loop(chunks // 2, chunks, input_grads, 0)
    fill(WGRID, acc_t[:, :width].T, grid_scale)
    advance(WGRID)
    fill(WAGG, acc_t[:, width:].T, grid_scale)
    advance(WAGG)
    lax.fori_loop(0, chunks, agg_grads, 0)
    advance(WGRID, WAGG)

    total[...] = jnp.zeros_like(total)

    def backward(outer, carry):
        for inner in range(UNROLL):
            r = outer * UNROLL + inner
            keep = entry("bwd_same", r).astype(f32)
            value = total[...] * keep + mm_tn(mask_v[entry("bwd_slot", r)], dagg_v[entry("bwd_grid", r)])
            total[...] = value
            runs[r] = (value * edge_scale * slope[entry("bwd_mesh", r)]).astype(bf16)
        return carry

    lax.fori_loop(0, slots // UNROLL, backward, 0)
    advance(WOUT)
    for b in range(ds_v.shape[0] // block):
        ds_v[pl.ds(b * block, block), :] = looked_up("mesh_last", b)
    piece = rows // PIECES
    returns = [
        pltpu.make_async_remote_copy(
            src_ref=ds_v.at[pl.ds(2 * slot * rows + p * piece, piece)],
            dst_ref=ds_in.at[slot, pl.ds(p * piece, piece)],
            send_sem=halo_send.at[2 + 2 * p + slot],
            recv_sem=halo_recv.at[2 + 2 * p + slot],
            device_id=to,
            device_id_type=MESH,
        )
        for p in range(PIECES)
        for slot, to in enumerate((left, right))
    ]

    def give_back(p):
        for copy in returns[2 * p : 2 * p + 2]:
            copy.start()

    give_back(0)
    fill(SEND, mm_tn(src_v[...], ds_v[...]), send_scale)
    advance(SEND)

    def finish_chunk(c):
        part = pl.ds(c * CHUNK, CHUNK)
        dec = grid_v[part, :].astype(f32) + mm(hidden_v[part, :], wout_v[...])
        hidden_v[part, :] = dec.astype(bf16)
        out = pltpu.make_async_copy(hidden_v.at[part], dec_hbm.at[part], out_sem.at[0, c])
        out.start()
        gg = cot_v[part, :].astype(f32) + mm_nt(dpre_v[part, :], wgrid_v[...])
        dpre_v[part, :] = gg.astype(bf16)
        out_g = pltpu.make_async_copy(dpre_v.at[part], gg_hbm.at[part], out_sem.at[1, c])
        out_g.start()
        return [out, out_g]

    for c in range(chunks):
        outs += finish_chunk(c)
        if c == 1:
            advance(SEND)
        if c == 4:
            advance(WOUT)
            give_back(1)
    advance(WGRID, WAGG)
    give_back(2)
    advance(SEND)
    give_back(3)
    advance(WGRID, WAGG)
    advance(WOUT)
    advance(SEND)
    advance(WOUT)
    advance(WGRID, WAGG)
    for copy in returns:
        copy.wait()
    dsender = ds_v[pl.ds(rows, rows), :].astype(f32) + ds_in[0].astype(f32) + ds_in[1].astype(f32)
    gm_v[...] = mm_nt(dsender.astype(bf16), wsend_v[...]).astype(bf16)
    out = pltpu.make_async_copy(gm_v, gm_hbm, end_sem.at[4])
    out.start()
    outs.append(out)
    for _ in range(6):
        advance(SEND, WGRID, WAGG, WOUT)
    for copy in outs:
        copy.wait()
    for copy in started:
        copy.wait_send()


def decoder_call(groups, send_scale, grid_scale, *arrays):
    mesh_latent, grid_latent, _, tile_mask = arrays[3:7]
    slots, block, _ = tile_mask.shape
    rows, width = mesh_latent.shape
    grid_rows = grid_latent.shape[0]
    full = width * width // 128
    half = full // 2
    hspec = pl.BlockSpec(memory_space=pltpu.HBM)
    dma = pltpu.SemaphoreType.DMA
    weight = VMEM((width, width), bf16)
    node = VMEM((grid_rows, width), bf16)
    chunks = grid_rows // CHUNK
    return pl.pallas_call(
        functools.partial(decoder_kernel, groups, send_scale, grid_scale),
        name="decoder",
        out_shape=[
            jax.ShapeDtypeStruct((grid_rows, width), bf16),
            jax.ShapeDtypeStruct((grid_rows, width), bf16),
            jax.ShapeDtypeStruct((rows, width), bf16),
            jax.ShapeDtypeStruct((4, full, 128), bf16),
        ],
        in_specs=[pl.BlockSpec(memory_space=pltpu.SMEM)] * 3 + [hspec] * 8,
        out_specs=[hspec] * 4,
        scratch_shapes=[
            node,
            node,
            VMEM((grid_rows, width), f32),
            node,
            node,
            VMEM((grid_rows // block, block, width), bf16),
            VMEM((3 * rows, width), bf16),
            VMEM((3 * rows // block, block, width), bf16),
            VMEM((3 * rows // block, block, width), f32),
            VMEM((2, slots // 4, block, block), i32),
            VMEM((slots, block, block), bf16),
            weight,
            weight,
            weight,
            weight,
            VMEM((slots + 1, block, width), bf16),
            VMEM((block, width), f32),
            VMEM((width, width), f32),
            VMEM((width, 2 * width), f32),
            VMEM((3 * rows, width), bf16),
            VMEM((2, rows, width), bf16),
            VMEM((4, full, 128), bf16),
            VMEM((4, full, 128), bf16),
            VMEM((4, half, 128), bf16),
            VMEM((4, len(PLANE), half // 16, 128), bf16),
            VMEM((4, 4, half // 16, 128), bf16),
            VMEM((rows, width), bf16),
            VMEM((slots, 128), i32),
            VMEM((slots, 128), i32),
            VMEM((len(ROWS), 128), i32),
            pltpu.SMEM((len(ROWS), 128), i32),
            dma((5,)),
            dma((2, chunks)),
            dma((2,)),
            dma,
            dma((2, chunks)),
            dma((5,)),
            dma((2 + 2 * PIECES,)),
            dma((2 + 2 * PIECES,)),
            dma((4 * SEMS,)),
            dma((4 * SEMS,)),
        ],
        compiler_params=pltpu.CompilerParams(
            collective_id=0, has_side_effects=True, vmem_limit_bytes=61 * MIB
        ),
    )(*arrays)


def finish_kernel(dec_in, gg_in, gm_in, packed_hbm, dec, gg, gm, g0, g1, g2, g3, packed, grads, copy_sem, in_sem, out_sem):
    width = grads.shape[1]
    loads = [pltpu.make_async_copy(packed_hbm.at[i], packed.at[i], in_sem.at[i]) for i in range(4)]
    for load in loads:
        load.start()
    moves = [pltpu.make_async_copy(gm_in, gm, copy_sem.at[2 * PIECES])]
    piece = dec.shape[0] // PIECES
    for p in range(PIECES):
        part = pl.ds(p * piece, piece)
        moves.append(pltpu.make_async_copy(dec_in.at[part], dec.at[part], copy_sem.at[2 * p]))
        moves.append(pltpu.make_async_copy(gg_in.at[part], gg.at[part], copy_sem.at[2 * p + 1]))
    for move in moves:
        move.start()
    for index, out in enumerate((g0, g1, g2, g3)):
        loads[index].wait()
        for c in range(width // 128):
            grads[index, :, c * 128 : (c + 1) * 128] = packed[index, pl.ds(c * width, width), :].astype(f32)
        move = pltpu.make_async_copy(grads.at[index], out, out_sem.at[index])
        move.start()
        moves.append(move)
    for move in moves:
        move.wait()


def finish_call(decoded, grad_grid, grad_mesh, packed):
    width = grad_grid.shape[1]
    hspec = pl.BlockSpec(memory_space=pltpu.HBM)
    dma = pltpu.SemaphoreType.DMA
    return pl.pallas_call(
        finish_kernel,
        name="finish",
        out_shape=[jax.ShapeDtypeStruct(x.shape, x.dtype) for x in (decoded, grad_grid, grad_mesh)]
        + [jax.ShapeDtypeStruct((width, width), f32)] * 4,
        in_specs=[hspec] * 4,
        out_specs=[hspec] * 7,
        scratch_shapes=[
            VMEM(packed.shape, bf16),
            VMEM((4, width, width), f32),
            dma((2 * PIECES + 1,)),
            dma((4,)),
            dma((4,)),
        ],
        compiler_params=pltpu.CompilerParams(vmem_limit_bytes=32 * MIB),
    )(decoded, grad_grid, grad_mesh, packed)


def per_device(
    mesh_latent,
    grid_latent,
    w_send,
    w_grid,
    w_agg,
    w_out,
    cotangent,
    tile_mesh,
    tile_grid,
    tile_count,
    tile_mask,
):
    mesh_rows = mesh_latent.shape[0]
    grid_rows = grid_latent.shape[0]
    groups = lax.axis_size("grid")
    devices_all = lax.axis_size("mesh") * groups
    send_scale = (mesh_rows * devices_all) ** (-0.5)
    grid_scale = (grid_rows * devices_all) ** (-0.5)
    results = decoder_call(
        groups,
        send_scale,
        grid_scale,
        tile_mesh,
        tile_grid,
        tile_count,
        mesh_latent,
        grid_latent,
        cotangent,
        tile_mask,
        w_send,
        w_grid,
        w_agg,
        w_out,
    )
    decoded, grad_grid, grad_mesh, *grads = finish_call(*results)
    return (decoded, grad_grid, grad_mesh, grads[SEND], grads[WGRID], grads[WAGG], grads[WOUT])


def solution(mesh):
    both = ("mesh", "grid")
    return jax.shard_map(
        per_device,
        mesh=mesh,
        in_specs=(
            P(both, None),
            P(both, None),
            P(),
            P(),
            P(),
            P(),
            P(both, None),
            P(both),
            P(both),
            P(both),
            P(both, None, None),
        ),
        out_specs=(P(both, None), P(both, None), P(both, None), P(), P(), P(), P()),
        check_vma=False,
    )
```

time: 102 us -> 101 us (level)
  Pallas kernels: 87 us -> 92 us
  local copies, waits for them, and re-layouts: 10.9 us -> 7 us
  other arithmetic: 2.91 us -> 0 us
    pallas_call x1, Pallas kernels: 2.36 us -> 5.02 us  [finish_call(): pl.pallas_call(finish_kernel, name='finish', out_shape=[jax.ShapeDtypeStr...]
    pallas_call x1, Pallas kernels: 84.6 us -> 87 us  [decoder_call(): pl.pallas_call(functools.partial(decoder_kernel, groups, send_scale, grid...]
    unnamed x9 -> x8, local copies, waits for them, and re-layouts: 9.03 us -> 7 us
    convert_element_type x2 -> x0, other arithmetic: 1.44 us -> none  [tile_tables(): value.astype(i32)]
    slice x2 -> x0, local copies, waits for them, and re-layouts: 1.17 us -> none  [the longest x1 0.59 us: tile_tables(): jnp.roll(sorted_mesh, 1)]
where the time goes in v1:
time: 101 us; the launch traced here: 100 us
  Pallas kernels  92 us (91%)
  local copies, waits for them, and re-layouts  7 us (7%)
  between operations  1.46 us (1%)
    pallas_call x1, Pallas kernels, decoder_call(): pl.pallas_call(functools.partial(decoder_kernel, groups, send_scale, grid...  87 us
    unnamed x8, local copies, waits for them, and re-layouts  7 us
    pallas_call x1, Pallas kernels, finish_call(): pl.pallas_call(finish_kernel, name='finish', out_shape=[jax.ShapeDtypeStr...  5.02 us

profile of v1, /device:TPU:1, one launch (start us, length us, event | category | flops | bytes accessed | tf_op | source)
XLA Modules:
  0.0 100.4 jit_solution(16820097594294396644)
XLA Ops:
  1.3 87.0 %decoder.1 = (bf16[4096,512]{1,0:T(8,128)(2,1)}, bf16[4096,512]{1,0:T(8,128)(2,1)}, bf16[512,512]{1,0:T(8,128)(2,1)}, bf16[4,2048,128]{2,1,0:T(8,128)(2,1)}) custom-call(s32[48]{0:T(128)} %tmesh.1, s32[48]{0:T(128)} %tgrid.1, s32[1]{0:T(128)S(6)} %copy.18.tcount, bf16[512,512]{1,0:T(8,128)(2,1)} %mesh_hbm.1, bf16[4096,512]{1,0:T(8,128)(2,1)} %grid_hbm.1, ...), custom_call_target="tpu_custom_call" | custom-call | tf_op jit(solution)/shard_map/decoder/pallas_call | solution.py:506
  88.2 0.0 copy-start
  88.3 2.2 %copy-done = bf16[4096,512]{1,0:T(8,128)(2,1)S(1)} copy-done((bf16[4096,512]{1,0:T(8,128)(2,1)S(1)}, bf16[4096,512]{1,0:T(8,128)(2,1)}, u32[]{:S(2)}) %copy-start) | copy-done | bytes 4194328
  90.4 0.0 copy-start.1
  90.4 2.2 %copy-done.1 = bf16[4096,512]{1,0:T(8,128)(2,1)S(1)} copy-done((bf16[4096,512]{1,0:T(8,128)(2,1)S(1)}, bf16[4096,512]{1,0:T(8,128)(2,1)}, u32[]{:S(2)}) %copy-start.1) | copy-done | bytes 4194328
  92.6 0.0 copy-start.2
  92.6 1.6 %copy-done.2 = bf16[4,2048,128]{2,1,0:T(8,128)(2,1)S(1)} copy-done((bf16[4,2048,128]{2,1,0:T(8,128)(2,1)S(1)}, bf16[4,2048,128]{2,1,0:T(8,128)(2,1)}, u32[]{:S(2)}) %copy-start.2) | copy-done | bytes 2097176
  94.2 0.0 copy-start.3
  94.2 1.0 %copy-done.3 = bf16[512,512]{1,0:T(8,128)(2,1)S(1)} copy-done((bf16[512,512]{1,0:T(8,128)(2,1)S(1)}, bf16[512,512]{1,0:T(8,128)(2,1)}, u32[]{:S(2)}) %copy-start.3) | copy-done | bytes 524312
  95.3 5.0 %finish.1 = (bf16[4096,512]{1,0:T(8,128)(2,1)}, bf16[4096,512]{1,0:T(8,128)(2,1)}, bf16[512,512]{1,0:T(8,128)(2,1)}, f32[512,512]{1,0:T(8,128)}, f32[512,512]{1,...) custom-call(bf16[4096,512]{1,0:T(8,128)(2,1)S(1)} %copy-done, bf16[4096,512]{1,0:T(8,128)(2,1)S(1)} %copy-done.1, ...), custom_call_target="tpu_custom_call" | custom-call | tf_op jit(solution)/shard_map/finish/pallas_call | solution.py:594
Async XLA Ops:
  88.2 2.2 %copy-start = (bf16[4096,512]{1,0:T(8,128)(2,1)S(1)}, bf16[4096,512]{1,0:T(8,128)(2,1)}, u32[]{:S(2)}) copy-start(bf16[4096,512]{1,0:T(8,128)(2,1)} %get-tuple-element.18.dec_in) | copy-start | bytes 12582916
  90.4 2.2 %copy-start.1 = (bf16[4096,512]{1,0:T(8,128)(2,1)S(1)}, bf16[4096,512]{1,0:T(8,128)(2,1)}, u32[]{:S(2)}) copy-start(bf16[4096,512]{1,0:T(8,128)(2,1)} %get-tuple-element.19.gg_in) | copy-start | bytes 12582916
  92.6 1.6 %copy-start.2 = (bf16[4,2048,128]{2,1,0:T(8,128)(2,1)S(1)}, bf16[4,2048,128]{2,1,0:T(8,128)(2,1)}, u32[]{:S(2)}) copy-start(bf16[4,2048,128]{2,1,0:T(8,128)(2,1)} %get-tuple-element.21.packed_hbm) | copy-start | bytes 6291460
  94.2 1.0 %copy-start.3 = (bf16[512,512]{1,0:T(8,128)(2,1)S(1)}, bf16[512,512]{1,0:T(8,128)(2,1)}, u32[]{:S(2)}) copy-start(bf16[512,512]{1,0:T(8,128)(2,1)} %get-tuple-element.20.gm_in) | copy-start | bytes 1572868

commit v2 on v1

--- a/solution.py
+++ b/solution.py
@@ -93,6 +93,7 @@
 PLANE = tuple((dy, dz) for dy in range(4) for dz in range(4) if (dy, dz) != (0, 0))
 SEND, WGRID, WAGG, WOUT = 3, 1, 2, 0
 SEMS = 35
+ROUTES = {WOUT: ("z", "y"), WGRID: ("y", "z"), WAGG: ("z", "y"), SEND: "plane"}
 PIECES = 4
 
 
@@ -133,15 +134,17 @@
     runs,
     total,
     acc_out,
-    acc_t,
+    acc_in,
     ds_v,
     ds_in,
     packed,
     final,
     r0,
     r1,
+    r2,
     r3,
-    gm_v,
+    a1,
+    b1,
     mesh_col,
     grid_col,
     table_v,
@@ -156,6 +159,7 @@
     halo_recv,
     send_sem,
     recv_sem,
+    near_sem,
 ):
     slots, block, _ = mask_v.shape
     rows, width = mesh_hbm.shape
@@ -176,11 +180,19 @@
     def along_x(d):
         return (row, at["y"] * 4 + lax.rem(at["x"] + d, 4))
 
+    def tell_near(stage):
+        for other in near:
+            pl.semaphore_signal(near_sem.at[stage], inc=1, device_id=other, device_id_type=MESH)
+
+    def hear_near(stage):
+        pl.semaphore_wait(near_sem.at[stage], len(near))
+
     def entry(name, index):
         return table[ROWS[name], index]
 
     barrier = pltpu.get_barrier_semaphore()
-    others = [left, right, sibling] + [along_x(d) for d in (1, 2, 3)] + [plane(*step)[0] for step in PLANE]
+    near = [along_x(1), along_x(3)] + [plane(*step)[0] for step in ((1, 0), (3, 0), (0, 1), (0, 3))]
+    others = [left, right, sibling] + near
     for other in others:
         pl.semaphore_signal(barrier, inc=1, device_id=other, device_id_type=MESH)
     loads = [
@@ -227,6 +239,7 @@
     ]
     for copy in halos:
         copy.start()
+    tell_near(0)
     masks[1].start()
     for c in range(1, chunks):
         for copy in chunk_loads(c):
@@ -258,6 +271,8 @@
         slope[blocks] = grad.reshape(per_part, block, width)
 
     project(1)
+    hear_near(0)
+    tell_near(1)
     per_grid = grid_rows // block
     first = (row * groups + col - 1) * per_part
     tile_tables(tmesh, tgrid, tcount, first, per_grid, 3 * per_part, mesh_col, grid_col, table_v)
@@ -274,8 +289,10 @@
         lax.fori_loop(0, quarter, convert, 0)
         if q + 2 < len(masks):
             masks[q + 2].start()
+    hear_near(1)
+    tell_near(2)
     acc_out[...] = jnp.zeros_like(acc_out)
-    acc_t[...] = jnp.zeros_like(acc_t)
+    acc_in[...] = jnp.zeros_like(acc_in)
     total[...] = jnp.zeros_like(total)
     runs[slots] = jnp.zeros((block, width), bf16)
     to_scalars.wait()
@@ -283,6 +300,7 @@
         copy.wait()
     project(0)
     project(2)
+    hear_near(2)
 
     def forward(outer, carry):
         for inner in range(UNROLL):
@@ -305,25 +323,20 @@
 
     def node_mlp(c, carry):
         part = pl.ds(pl.multiple_of(c * CHUNK, CHUNK), CHUNK)
-        act, grad = silu_parts(pre_v[part, :] + mm(agg_chunk(c), wagg_v[...]))
+        agg = agg_chunk(c)
+        act, grad = silu_parts(pre_v[part, :] + mm(agg, wagg_v[...]))
         hidden = act.astype(bf16)
         hidden_v[part, :] = hidden
-        dpre_v[part, :] = (dpre_v[part, :].astype(f32) * grad).astype(bf16)
+        dpre = (dpre_v[part, :].astype(f32) * grad).astype(bf16)
+        dpre_v[part, :] = dpre
         acc_out[...] += mm_tn(hidden, cot_v[part, :])
-        return carry
-
-    def input_grads(c, carry):
-        part = pl.ds(pl.multiple_of(c * CHUNK, CHUNK), CHUNK)
-        dpre_t = dpre_v[part, :].T
-        acc_t[:, :width] += mm(dpre_t, grid_v[part, :])
-        acc_t[:, width:] += mm(dpre_t, agg_chunk(c))
-        return carry
-
-    def agg_grads(c, carry):
-        part = pl.ds(pl.multiple_of(c * CHUNK, CHUNK), CHUNK)
-        dagg = mm_nt(dpre_v[part, :], wagg_v[...]).astype(bf16)
+        acc_in[:, :width] += mm_tn(grid_v[part, :], dpre)
+        acc_in[:, width:] += mm_tn(agg, dpre)
+        dagg = mm_nt(dpre, wagg_v[...]).astype(bf16)
         dagg_v[pl.ds(c * per_chunk, per_chunk)] = dagg.reshape(per_chunk, block, width)
         return carry
+
+    lax.fori_loop(0, chunks, node_mlp, 0, unroll=2)
 
     half = packed.shape[1] // 2
     size = half // 16
@@ -355,6 +368,84 @@
             copy.wait_recv()
 
     def stream(i):
+        return plane_stream(i) if ROUTES[i] == "plane" else axes_stream(i)
+
+    def along(axis, d):
+        return plane(d, 0)[0] if axis == "y" else plane(0, d)[0]
+
+    def meet(i, chunk, sem):
+        me = at["x"]
+        r3[i, me] = chunk.astype(bf16)
+        return [go(r3.at[i, me], r3.at[i, me], sem + d - 1, along_x(d)) for d in (1, 2, 3)]
+
+    def met(i, where):
+        value = r3[i, 0].astype(f32)
+        for k in range(1, 4):
+            value = value + r3[i, k].astype(f32)
+        final[i, pl.ds(where, size), :] = value.astype(bf16)
+
+    def finished(i, sem):
+        window = final.at[i, pl.ds(mine, half)]
+        return [go(window, window, sem, sibling)]
+
+    def store(i):
+        out = pltpu.make_async_copy(final.at[i], final_hbm.at[i], end_sem.at[i])
+        out.start()
+        outs.append(out)
+
+    def axes_stream(i):
+        sem = i * SEMS
+        axis_a, axis_b = ROUTES[i]
+        wide = 4 * size
+        copies = [go(packed.at[i, pl.ds(theirs, half)], r0.at[i], sem, sibling)]
+        yield
+        arrived(copies)
+        off_a = pl.multiple_of(at[axis_a] * wide, wide)
+        off_b = pl.multiple_of(at[axis_b] * size, size)
+        base = pl.multiple_of(mine + off_a, wide)
+        band = packed[i, pl.ds(base, wide), :].astype(f32) + r0[i, pl.ds(off_a, wide), :].astype(f32)
+        r0[i] = (packed[i, pl.ds(mine, half), :].astype(f32) + r0[i].astype(f32)).astype(bf16)
+        a1[i] = band
+        copies = []
+        for d in (1, 2, 3):
+            window = pl.ds(pl.multiple_of(lax.rem(at[axis_a] + d, 4) * wide, wide), wide)
+            slot = r2.at[i, d - 1]
+            copies.append(go(r0.at[i, window], slot, sem + d, along(axis_a, d)))
+        yield
+        arrived(copies)
+        band = a1[i]
+        for d in range(3):
+            band = band + r2[i, d].astype(f32)
+        a1[i] = band
+        b1[i] = band.astype(bf16)
+        copies = []
+        for d in (1, 2, 3):
+            window = pl.ds(pl.multiple_of(lax.rem(at[axis_b] + d, 4) * size, size), size)
+            copies.append(go(b1.at[i, window], r1.at[i, 11 + d], sem + 3 + d, along(axis_b, d)))
+        yield
+        arrived(copies)
+        chunk = a1[i, pl.ds(off_b, size), :]
+        for d in (1, 2, 3):
+            chunk = chunk + r1[i, 11 + d].astype(f32)
+        copies = meet(i, chunk, sem + 7)
+        yield
+        arrived(copies)
+        here = pl.multiple_of(base + off_b, size)
+        met(i, here)
+        window = final.at[i, pl.ds(here, size)]
+        copies = [go(window, window, sem + 9 + d, along(axis_b, d)) for d in (1, 2, 3)]
+        yield
+        arrived(copies)
+        window = final.at[i, pl.ds(base, wide)]
+        copies = [go(window, window, sem + 12 + d, along(axis_a, d)) for d in (1, 2, 3)]
+        yield
+        arrived(copies)
+        copies = finished(i, sem + 34)
+        yield
+        arrived(copies)
+        store(i)
+
+    def plane_stream(i):
         sem = i * SEMS
         copies = [go(packed.at[i, pl.ds(theirs, half)], r0.at[i], sem, sibling)]
         yield
@@ -370,26 +461,18 @@
         arrived(copies)
         for k in range(len(PLANE)):
             chunk = chunk + r1[i, k].astype(f32)
-        me = at["x"]
-        r3[i, me] = chunk.astype(bf16)
-        copies = [go(r3.at[i, me], r3.at[i, me], sem + 15 + d, along_x(d)) for d in (1, 2, 3)]
-        yield
-        arrived(copies)
-        value = r3[i, 0].astype(f32)
-        for k in range(1, 4):
-            value = value + r3[i, k].astype(f32)
-        final[i, pl.ds(own, size), :] = value.astype(bf16)
+        copies = meet(i, chunk, sem + 16)
+        yield
+        arrived(copies)
+        met(i, own)
         window = final.at[i, pl.ds(own, size)]
         copies = [go(window, window, sem + 19 + k, plane(*step)[0]) for k, step in enumerate(PLANE)]
         yield
         arrived(copies)
-        window = final.at[i, pl.ds(mine, half)]
-        copies = [go(window, window, sem + 34, sibling)]
-        yield
-        arrived(copies)
-        out = pltpu.make_async_copy(final.at[i], final_hbm.at[i], end_sem.at[i])
-        out.start()
-        outs.append(out)
+        copies = finished(i, sem + 34)
+        yield
+        arrived(copies)
+        store(i)
 
     outs = []
     streams = [stream(i) for i in range(4)]
@@ -398,18 +481,12 @@
         for i in which:
             next(streams[i], None)
 
-    lax.fori_loop(0, chunks, node_mlp, 0)
     fill(WOUT, acc_out[...], grid_scale)
     advance(WOUT)
-    lax.fori_loop(0, chunks // 2, input_grads, 0)
-    advance(WOUT)
-    lax.fori_loop(chunks // 2, chunks, input_grads, 0)
-    fill(WGRID, acc_t[:, :width].T, grid_scale)
+    fill(WGRID, acc_in[:, :width], grid_scale)
     advance(WGRID)
-    fill(WAGG, acc_t[:, width:].T, grid_scale)
+    fill(WAGG, acc_in[:, width:], grid_scale)
     advance(WAGG)
-    lax.fori_loop(0, chunks, agg_grads, 0)
-    advance(WGRID, WAGG)
 
     total[...] = jnp.zeros_like(total)
 
@@ -422,8 +499,10 @@
             runs[r] = (value * edge_scale * slope[entry("bwd_mesh", r)]).astype(bf16)
         return carry
 
-    lax.fori_loop(0, slots // UNROLL, backward, 0)
-    advance(WOUT)
+    for first_step, which in enumerate((WOUT, WGRID, WAGG)):
+        lax.fori_loop(first_step, first_step + 1, backward, 0)
+        advance(which)
+    lax.fori_loop(3, slots // UNROLL, backward, 0)
     for b in range(ds_v.shape[0] // block):
         ds_v[pl.ds(b * block, block), :] = looked_up("mesh_last", b)
     piece = rows // PIECES
@@ -464,23 +543,24 @@
         outs += finish_chunk(c)
         if c == 1:
             advance(SEND)
-        if c == 4:
-            advance(WOUT)
+        if c == 2:
+            advance(WOUT, WGRID, WAGG)
+        if c == 3:
             give_back(1)
-    advance(WGRID, WAGG)
+    advance(WOUT, WGRID, WAGG)
+    advance(WOUT, WGRID, WAGG)
     give_back(2)
     advance(SEND)
+    advance(WOUT, WGRID, WAGG)
     give_back(3)
-    advance(WGRID, WAGG)
-    advance(WOUT)
     advance(SEND)
-    advance(WOUT)
-    advance(WGRID, WAGG)
+    advance(WOUT, WGRID, WAGG)
+    advance(SEND)
     for copy in returns:
         copy.wait()
     dsender = ds_v[pl.ds(rows, rows), :].astype(f32) + ds_in[0].astype(f32) + ds_in[1].astype(f32)
-    gm_v[...] = mm_nt(dsender.astype(bf16), wsend_v[...]).astype(bf16)
-    out = pltpu.make_async_copy(gm_v, gm_hbm, end_sem.at[4])
+    ds_in[0] = mm_nt(dsender.astype(bf16), wsend_v[...]).astype(bf16)
+    out = pltpu.make_async_copy(ds_in.at[0], gm_hbm, end_sem.at[4])
     out.start()
     outs.append(out)
     for _ in range(6):
@@ -524,7 +604,7 @@
             VMEM((3 * rows, width), bf16),
             VMEM((3 * rows // block, block, width), bf16),
             VMEM((3 * rows // block, block, width), f32),
-            VMEM((2, slots // 4, block, block), i32),
+            VMEM((2, slots // 8, block, block), i32),
             VMEM((slots, block, block), bf16),
             weight,
             weight,
@@ -540,8 +620,10 @@
             VMEM((4, full, 128), bf16),
             VMEM((4, half, 128), bf16),
             VMEM((4, len(PLANE), half // 16, 128), bf16),
+            VMEM((4, 3, half // 4, 128), bf16),
             VMEM((4, 4, half // 16, 128), bf16),
-            VMEM((rows, width), bf16),
+            VMEM((4, half // 4, 128), f32),
+            VMEM((4, half // 4, 128), bf16),
             VMEM((slots, 128), i32),
             VMEM((slots, 128), i32),
             VMEM((len(ROWS), 128), i32),
@@ -556,9 +638,10 @@
             dma((2 + 2 * PIECES,)),
             dma((4 * SEMS,)),
             dma((4 * SEMS,)),
+            pltpu.SemaphoreType.REGULAR((3,)),
         ],
         compiler_params=pltpu.CompilerParams(
-            collective_id=0, has_side_effects=True, vmem_limit_bytes=61 * MIB
+            collective_id=0, has_side_effects=True, vmem_limit_bytes=62 * MIB
         ),
     )(*arrays)
 
@@ -605,7 +688,7 @@
             dma((4,)),
             dma((4,)),
         ],
-        compiler_params=pltpu.CompilerParams(vmem_limit_bytes=32 * MIB),
+        compiler_params=pltpu.CompilerParams(vmem_limit_bytes=62 * MIB),
     )(decoded, grad_grid, grad_mesh, packed)
 
 

time: 101 us -> 358 us (3.54)
  Pallas kernels: 92 us -> 356 us
  local copies, waits for them, and re-layouts: 7 us -> 0 us
    pallas_call x1, Pallas kernels: 5.02 us -> 271 us  [finish_call(): pl.pallas_call(finish_kernel, name='finish', out_shape=[jax.ShapeDtypeStr...]
    unnamed x8 -> x0, local copies, waits for them, and re-layouts: 7 us -> none
where the time goes in v2:
time: 358 us
  Pallas kernels  356 us (99%)
    pallas_call x1, Pallas kernels, finish_call(): pl.pallas_call(finish_kernel, name='finish', out_shape=[jax.ShapeDtypeStr...  271 us
    pallas_call x1, Pallas kernels, decoder_call(): pl.pallas_call(functools.partial(decoder_kernel, groups, send_scale, grid...  84.8 us

profile of v2, /device:TPU:1, one launch (start us, length us, event | category | flops | bytes accessed | tf_op | source)
XLA Modules:
  0.0 357.6 jit_solution(8669675554894027204)
XLA Ops:
  1.3 84.8 %decoder.1 = (bf16[4096,512]{1,0:T(8,128)(2,1)}, bf16[4096,512]{1,0:T(8,128)(2,1)}, bf16[512,512]{1,0:T(8,128)(2,1)}, bf16[4,2048,128]{2,1,0:T(8,128)(2,1)}) custom-call(s32[48]{0:T(128)} %tmesh.1, s32[48]{0:T(128)} %tgrid.1, s32[1]{0:T(128)S(6)} %copy.18.tcount, bf16[512,512]{1,0:T(8,128)(2,1)} %mesh_hbm.1, bf16[4096,512]{1,0:T(8,128)(2,1)} %grid_hbm.1, ...), custom_call_target="tpu_custom_call" | custom-call | tf_op jit(solution)/shard_map/decoder/pallas_call | solution.py:586
  86.1 271.3 %finish.1 = (bf16[4096,512]{1,0:T(8,128)(2,1)}, bf16[4096,512]{1,0:T(8,128)(2,1)}, bf16[512,512]{1,0:T(8,128)(2,1)}, f32[512,512]{1,0:T(8,128)}, f32[512,512]{1,...) custom-call(bf16[4096,512]{1,0:T(8,128)(2,1)} %get-tuple-element.18.dec_in, ...), custom_call_target="tpu_custom_call" | custom-call | tf_op jit(solution)/shard_map/finish/pallas_call | solution.py:677
